TPU v7x, 128 devices: a whole 4x4x4 slice. The times are simulated.
128 devices in a mesh: loop: 32 (over z_lo, y, x), grp: 4 (over z_hi, core).
Axes of the slice: x: 4, y: 4, z: 4 (z_hi: 2, z_lo: 2; z = z_hi * 2 + z_lo), core: 2. Of those that a mesh axis runs over, the one named last changes fastest.
Arguments:
- inputs: bfloat16 [2, 128, 4096], P(None, 'grp', 'loop'), may hold values from -6 to 6
- in_weight: bfloat16 [4096, 12304], P('loop', 'grp'), may hold values from -0.09375 to 0.09375
- gate_bias: float32 [2, 8], replicated, may hold values from -2 to 104, as said below
- memory: float32 [128, 8, 256, 512], P(('grp', 'loop')), may hold values from -6 to 6
- normalizer: float32 [128, 8, 256], P(('grp', 'loop')), may hold values from -6 to 6
- stabilizer: float32 [128, 8], P(('grp', 'loop')), may hold values from 0 to 4
- out_gain: float32 [4096], replicated, may hold values from 0.5 to 1.5
- out_weight: bfloat16 [4096, 4096], P(None, 'loop'), may hold values from -0.09375 to 0.09375
Outputs:
- mixed_out: bfloat16 [2, 128, 4096], P(None, 'grp', 'loop')
- memory_out: float32 [128, 8, 256, 512], P(('grp', 'loop'))
- normalizer_out: float32 [128, 8, 256], P(('grp', 'loop'))
- stabilizer_out: float32 [128, 8], P(('grp', 'loop'))
Inputs may be any that keep to these rules, and one draw needn't show every extreme that they name: `gate_bias`: row 0 holds the input gates' biases, row 1 the forget gates'.
All inputs are finite; a program needn't handle non-finite values.
Results may differ from a plain program's by a relative error of at most 0.005.
Values may be sent and summed in bfloat16 or wider, within the bound.
A program may use at most 64 MiB of HBM per device.

v0:
```python
import math

import jax
import jax.numpy as jnp
from jax import lax
from jax.sharding import PartitionSpec as P


def advance(current, step_row, gate_bias, out_gain):
    memory, normalizer, stabilizer = current
    requests = memory.shape[0]
    head_count = memory.shape[1]
    key_dim = memory.shape[2]
    value_dim = memory.shape[3]
    qk_width = head_count * key_dim
    model_width = head_count * value_dim
    queries = step_row[:, :qk_width].reshape(requests, head_count, key_dim)
    keys = (step_row[:, qk_width : 2 * qk_width] * (1.0 / math.sqrt(key_dim))).reshape(
        requests, head_count, key_dim
    )
    base = 2 * qk_width
    values = step_row[:, base : base + model_width].reshape(requests, head_count, value_dim)
    out_gate = step_row[:, base + model_width : base + 2 * model_width]
    gates = base + 2 * model_width
    admit_pre = step_row[:, gates : gates + head_count] + gate_bias[0]
    forget_pre = step_row[:, gates + head_count : gates + 2 * head_count] + gate_bias[1]
    log_forget = jax.nn.log_sigmoid(forget_pre)
    new_stabilizer = jnp.maximum(log_forget + stabilizer, admit_pre)
    forget = jnp.exp(log_forget + stabilizer - new_stabilizer)
    admit = jnp.exp(admit_pre - new_stabilizer)
    scaled_keys = admit[..., None] * keys
    memory = forget[..., None, None] * memory + scaled_keys[..., :, None] * values[..., None, :]
    normalizer = forget[..., None] * normalizer + scaled_keys
    numerator = jnp.einsum("rhk,rhkv->rhv", queries, memory, precision=lax.Precision.HIGHEST)
    denominator = jnp.maximum(jnp.abs(jnp.sum(queries * normalizer, -1)), 1.0)
    hidden = (numerator / denominator[..., None]).reshape(requests, model_width)
    rescale = lax.rsqrt(jnp.mean(hidden * hidden, -1, keepdims=True) + 1e-06)
    readout = (hidden * rescale * out_gain * jax.nn.sigmoid(out_gate)).astype(jnp.bfloat16)
    return ((memory, normalizer, new_stabilizer), readout)


def body(inputs, in_weight, gate_bias, memory, normalizer, stabilizer, out_gain, out_weight):
    loop_count = lax.axis_size("loop")
    group_count = lax.axis_size("grp")
    group_requests = inputs.shape[1]
    own_requests = group_requests // loop_count

    def sum_terms(gathered):
        shaped = gathered.reshape(gathered.shape[0], group_count, group_requests, gathered.shape[2])
        return jnp.einsum("sgrd,dc->rgsc", shaped, in_weight, preferred_element_type=jnp.float32)

    def arrange(restored):
        return jnp.swapaxes(
            restored.reshape(own_requests, restored.shape[2], restored.shape[3]), 0, 1
        )

    def project_out(shards):
        return jnp.einsum(
            "srd,dc->src", shards, out_weight, preferred_element_type=jnp.float32
        ).astype(jnp.bfloat16)

    def stepper(current, step_input):
        gathered_step = lax.all_gather(step_input[None], "grp", axis=1, tiled=True)
        owned_step = lax.psum_scatter(
            sum_terms(gathered_step), "loop", scatter_dimension=0, tiled=True
        )
        step_row = arrange(
            lax.all_to_all(owned_step, "grp", split_axis=1, concat_axis=3, tiled=True)
        )[0]
        updated, readout = advance(current, step_row, gate_bias, out_gain)
        emitted = project_out(lax.all_gather(readout[None], "loop", axis=1, tiled=True))[0]
        return (updated, emitted)

    finished, collected = lax.scan(stepper, (memory, normalizer, stabilizer), inputs)
    return (collected, finished[0], finished[1], finished[2])


def solution(mesh):
    in_specs = (
        P(None, "grp", "loop"),
        P("loop", "grp"),
        P(),
        P(("grp", "loop"), None, None, None),
        P(("grp", "loop"), None, None),
        P(("grp", "loop"), None),
        P(),
        P(None, "loop"),
    )
    out_specs = (
        P(None, "grp", "loop"),
        P(("grp", "loop"), None, None, None),
        P(("grp", "loop"), None, None),
        P(("grp", "loop"), None),
    )
    return jax.shard_map(body, mesh=mesh, in_specs=in_specs, out_specs=out_specs, check_vma=False)
```

profile of v0, /device:TPU:1, one launch (start us, length us, event | category | flops | bytes accessed | tf_op | source)
XLA Modules:
  0.0 846.8 jit_solution(10949651076655878922)
XLA Ops:
  7.2 0.0 copy-start
  7.2 0.0 copy-start.1
  7.2 0.0 copy-start.2
  7.2 0.0 copy-start.4
  7.2 0.0 copy-start.5
  7.2 0.0 copy-start.6
  7.2 0.0 copy-start.8
  7.2 0.0 copy-start.10
  7.2 4.8 copy.60
  12.0 0.0 copy-done
  12.1 827.2 %while.16 = (s32[]{:T(128)}, f32[1,8,256,512]{3,2,1,0:T(8,128)}, f32[1,8,256]{2,1,0:T(8,128)S(1)}, f32[1,8]{1,0:T(1,128)S(1)}, bf16[2,32,128]{2,1,0:T(8,128)(2,1...) while((s32[]{:T(128)}, f32[1,8,256,512]{3,2,1,0:T(8,128)}, ...), condition=%wide.region_4.5_spmd, body=%wide.region_0.4_spmd.sunk | while | flops 150534784 | bytes 30560768 | solution.py:74
  12.1 0.0 all-reduce.5.cloned.1.call-start
  12.2 8.4 all_gather.7
  20.6 0.4 convolution_bitcast_fusion.2
  21.0 2.2 copy.36
  23.2 0.0 all-reduce.5.cloned.1.call-update
  23.2 0.6 dynamic-slice.6
  23.8 286.9 %all-reduce.5.cloned.1.call-done = f32[32,4,1,3076]{3,1,2,0:T(4,128)} async-done(((f32[32,4,1,3076]{3,1,2,0:T(4,128)}), f32[32,4,1,3076]{3,1,2,0:T(4,128)}) %all-reduce.5.cloned.1.call-update) | async-done | bytes 1574928 | tf_op jit(solution)/shard_map/while
  310.7 1.5 constant_dynamic-slice_fusion.5
  312.1 0.7 copy.37
  312.8 25.4 %all-to-all-start = ((f32[1,4,1,3076]{3,0,2,1:T(1,128)}), f32[1,4,1,3076]{3,0,2,1:T(1,128)S(1)}, u32[]{:S(2)}, u32[]{:S(2)}) async-start(f32[1,4,1,3076]{3,0,2,1:T(1,128)} %copy.37), calls=%async_computation | async-start | bytes 102400 | tf_op jit(solution)/shard_map/while/body/eval_jaxpr/all_to_all | solution.py:68
  338.3 4.7 all-to-all-done
  343.0 0.1 reduce.25
  343.1 0.1 reshape.201
  343.3 0.1 slice_reduce_fusion.5
  343.4 0.1 exponential_bitcast_fusion.4
  343.5 0.1 broadcast_multiply_fusion.2
  343.6 0.2 multiply_reduce_fusion.4
  343.8 4.8 multiply_add_fusion.4
  348.6 4.3 fusion.32
  352.8 0.7 multiply_reduce_fusion.5
  354.2 0.1 multiply_bitcast_fusion.2
  354.3 0.1 convert_bitcast_fusion.2
  354.4 66.5 %all-gather.3 = bf16[32,1,4096]{2,1,0:T(2,128)(2,1)S(1)} all-gather(bf16[1,1,4096]{2,1,0:T(2,128)(2,1)S(1)} %convert_bitcast_fusion.2), channel_id=2, replica_groups=mesh['loop'=32,'grp'=4] {'loop'}, dimensions={0}, use_global_device_ids=true | all-gather | bytes 270336 | tf_op jit(solution)/shard_map/while/body/eval_jaxpr/all_gather | solution.py:71
  420.8 0.5 fusion.33
  421.3 0.0 all-reduce.5.cloned.1.call-start
  421.4 21.5 %all_gather.7 = bf16[1,128,128]{2,1,0:T(8,128)(2,1)S(1)} all-gather(bf16[1,32,128]{2,1,0:T(8,128)(2,1)S(1)} %constant_dynamic-slice_fusion.4), channel_id=1, replica_groups=mesh['loop'=32,'grp'=4] {'grp'}, dimensions={1}, use_global_device_ids=true | all-gather | bytes 40960 | tf_op jit(solution)/shard_map/while/body/eval_jaxpr/all_gather | solution.py:63
  442.9 0.4 convolution_bitcast_fusion.2
  443.3 2.2 copy.36
  445.5 0.0 all-reduce.5.cloned.1.call-update
  445.6 0.6 dynamic-slice.6
  446.1 282.5 %all-reduce.5.cloned.1.call-done = f32[32,4,1,3076]{3,1,2,0:T(4,128)} async-done(((f32[32,4,1,3076]{3,1,2,0:T(4,128)}), f32[32,4,1,3076]{3,1,2,0:T(4,128)}) %all-reduce.5.cloned.1.call-update) | async-done | bytes 1574928 | tf_op jit(solution)/shard_map/while
  728.7 1.5 constant_dynamic-slice_fusion.5
  730.1 0.7 copy.37
  730.8 25.4 %all-to-all-start = ((f32[1,4,1,3076]{3,0,2,1:T(1,128)}), f32[1,4,1,3076]{3,0,2,1:T(1,128)S(1)}, u32[]{:S(2)}, u32[]{:S(2)}) async-start(f32[1,4,1,3076]{3,0,2,1:T(1,128)} %copy.37), calls=%async_computation | async-start | bytes 102400 | tf_op jit(solution)/shard_map/while/body/eval_jaxpr/all_to_all | solution.py:68
  756.2 4.7 all-to-all-done
  761.0 0.1 reduce.25
  761.1 0.1 reshape.201
  761.3 0.1 slice_reduce_fusion.5
  761.3 0.1 exponential_bitcast_fusion.4
  761.5 0.1 broadcast_multiply_fusion.2
  761.6 0.2 multiply_reduce_fusion.4
  761.8 4.8 multiply_add_fusion.4
  766.6 4.3 fusion.32
  770.8 0.7 multiply_reduce_fusion.5
  772.2 0.1 multiply_bitcast_fusion.2
  772.3 0.1 convert_bitcast_fusion.2
  772.4 66.5 %all-gather.3 = bf16[32,1,4096]{2,1,0:T(2,128)(2,1)S(1)} all-gather(bf16[1,1,4096]{2,1,0:T(2,128)(2,1)S(1)} %convert_bitcast_fusion.2), channel_id=2, replica_groups=mesh['loop'=32,'grp'=4] {'loop'}, dimensions={0}, use_global_device_ids=true | all-gather | bytes 270336 | tf_op jit(solution)/shard_map/while/body/eval_jaxpr/all_gather | solution.py:71
  838.8 0.5 fusion.33
  839.3 0.0 copy-start.3
  839.3 0.0 copy-start.7
  839.3 0.0 copy-start.9
  839.3 0.6 copy-done.3
  839.9 0.0 copy-done.9
  (27 shorter events, 0.2 us)
Async XLA Ops:
  7.2 4.8 copy-start
  7.2 4.8 copy-start.1
  7.2 4.8 copy-start.2
  7.2 4.8 copy-start.4
  7.2 4.8 copy-start.5
  7.2 4.8 copy-start.6
  7.2 4.8 copy-start.8
  7.2 4.8 copy-start.10
  12.1 298.6 %all-reduce.5.cloned.1.call-start = ((), (), s32[]{:S(2)}) async-start(), calls=%async_computation.1 | async-start | bytes 3276800 | tf_op jit(solution)/shard_map/while
  312.8 30.2 %all-to-all-start = ((f32[1,4,1,3076]{3,0,2,1:T(1,128)}), f32[1,4,1,3076]{3,0,2,1:T(1,128)S(1)}, u32[]{:S(2)}, u32[]{:S(2)}) async-start(f32[1,4,1,3076]{3,0,2,1:T(1,128)} %copy.37), calls=%async_computation | async-start | bytes 102400 | tf_op jit(solution)/shard_map/while/body/eval_jaxpr/all_to_all | solution.py:68
  421.3 307.3 %all-reduce.5.cloned.1.call-start = ((), (), s32[]{:S(2)}) async-start(), calls=%async_computation.1 | async-start | bytes 3276800 | tf_op jit(solution)/shard_map/while
  730.8 30.2 %all-to-all-start = ((f32[1,4,1,3076]{3,0,2,1:T(1,128)}), f32[1,4,1,3076]{3,0,2,1:T(1,128)S(1)}, u32[]{:S(2)}, u32[]{:S(2)}) async-start(f32[1,4,1,3076]{3,0,2,1:T(1,128)} %copy.37), calls=%async_computation | async-start | bytes 102400 | tf_op jit(solution)/shard_map/while/body/eval_jaxpr/all_to_all | solution.py:68
  839.3 0.6 copy-start.3
  839.3 0.6 copy-start.7
  839.3 0.6 copy-start.9
Sparse Core Ops, SparseCore 0:
  23.3 287.3 all-reduce.4
  445.7 282.9 all-reduce.4
where the time goes:
time: 863 us; the launch traced here: 847 us
  waiting for transfers between devices  579 us (67%)
  blocking collectives  163 us (19%)
  starting transfers between devices  51 us (6%)
  local copies, waits for them, and re-layouts  15.7 us (2%)
  between operations  14.1 us (2%)
  other arithmetic  12.3 us (1%)
  matrix products  10.2 us (1%)
    while x4, waiting for transfers between devices  569 us
    all_gather x2, blocking collectives, stepper(): lax.all_gather(readout[None], 'loop', axis=1, tiled=True)  133 us
    all_to_all x2, starting transfers between devices, stepper(): lax.all_to_all(owned_step, 'grp', split_axis=1, concat_axis=3, tiled=True)  50.9 us
    all_gather x2, blocking collectives, stepper(): gathered_step = lax.all_gather(step_input[None], 'grp', axis=1, tiled=True)  30 us
  transfers between devices with their start and end apart: 4, of which 4 were waited for; matrix products, arithmetic and copies ran while one was open for 0% of the time, Pallas kernels for 0%

commit v1 on v0

v1 whole, which is shorter than its diff:
```python
import jax
import jax.numpy as jnp
from jax import lax
from jax.experimental import pallas as pl
from jax.experimental.pallas import tpu as pltpu
from jax.sharding import PartitionSpec as P

MESH = pl.DeviceIdType.MESH
F32 = jnp.float32
BF16 = jnp.bfloat16


def split_low(value):
    return value - value.astype(BF16).astype(F32)


def to_column(row, shift=0):
    wide = jnp.broadcast_to(row, (8, row.shape[1]))
    lane = lax.broadcasted_iota(jnp.int32, wide.shape, 1)
    head = lax.broadcasted_iota(jnp.int32, wide.shape, 0)
    return jnp.sum(jnp.where(lane == head + shift, wide, 0.0), axis=1, keepdims=True)


def exchange_kernel(
    inputs_hbm, weight_hbm, bias_hbm, memory_hbm, norm_hbm, stab_hbm, gain_hbm, out_weight_hbm,
    mixed_ref, memory_out_ref, norm_out_ref, stab_out_ref,
    stage, memory, out_weight, bias, norm, stab, gain, rows_in, rows, tail, tail_f32, weights,
    send_f32, send, received, tiles, rolled, flat, numer, scaled, readout, gathered, gathered_f32, left,
    load_sem, own_sem, rows_send, rows_sem, ring_send, ring_sem, tail_send, tail_sem, w_send, w_sem, pass_send,
    pass_sem, sums_send, sums_recv, gather_send, gather_recv, ping_sem,
):
    loop_id = lax.axis_index("loop")
    grp_id = lax.axis_index("grp")
    x = lax.rem(loop_id, 4)
    y = lax.rem(lax.div(loop_id, 4), 4)
    z_lo = lax.div(loop_id, 16)
    z_hi = lax.div(grp_id, 2)
    core = lax.rem(grp_id, 2)

    def x_peer(o):
        return (z_lo * 16 + y * 4 + lax.rem(x + o, 4), grp_id)

    def y_peer(o):
        return (z_lo * 16 + lax.rem(y + o, 4) * 4 + x, grp_id)

    z_peer = (loop_id, (1 - z_hi) * 2 + core)
    other_lo = (1 - z_lo) * 16 + y * 4 + x
    z_near = [(other_lo, grp_id), (other_lo, (1 - z_hi) * 2 + core)]
    sibling = (loop_id, z_hi * 2 + 1 - core)

    loads = [
        pltpu.make_async_copy(src, dst, load_sem.at[i])
        for i, (src, dst) in enumerate((
            (inputs_hbm, rows_in.at[z_hi]),
            (weight_hbm, stage),
            (bias_hbm, bias),
            (stab_hbm, stab),
            (norm_hbm.at[0], norm),
            (gain_hbm, gain),
            (memory_hbm.at[0], memory),
            (out_weight_hbm, out_weight),
        ))
    ]
    for load in loads:
        load.start()

    barrier = pltpu.get_barrier_semaphore()
    peers = [x_peer(2), y_peer(2), z_peer] + z_near
    peers += [x_peer(1), x_peer(3), y_peer(1), y_peer(3), sibling]
    for peer in peers:
        pl.semaphore_signal(barrier, inc=1, device_id=peer, device_id_type=MESH)

    loads[0].wait()
    loads[1].wait()
    tail_f32[...] = jnp.zeros_like(tail_f32)
    tail_f32[0:4, :] = stage[3072:3076, :].astype(F32)
    tail[0] = pltpu.roll(tail_f32[...], grp_id * 4, 0).astype(BF16)

    pl.semaphore_wait(barrier, len(peers))

    def remote(src, dst, send_sem, recv_sem, peer):
        copy = pltpu.make_async_remote_copy(
            src_ref=src, dst_ref=dst, send_sem=send_sem, recv_sem=recv_sem, device_id=peer, device_id_type=MESH
        )
        copy.start()
        return copy

    def wait_bytes(ref, sem):
        pltpu.make_async_copy(ref, ref, sem).wait()

    rows_copy = remote(rows_in.at[z_hi], rows_in.at[z_hi], rows_send, rows_sem, z_peer)
    for peer in z_near:
        pl.semaphore_signal(ping_sem, inc=1, device_id=peer, device_id_type=MESH)
    tail_pair = remote(tail.at[0], tail.at[1], tail_send.at[0], tail_sem.at[0], sibling)

    def pieces(kind, holder, slot):
        wide = pl.ds(pl.multiple_of(kind * 1024 + holder * 256, 128), 256)
        one = pl.ds(pl.multiple_of(2048 + kind * 512 + holder * 128, 128), 128)
        deep = pl.ds(slot * 128, 128)
        return (
            (stage.at[wide], weights.at[kind, core, pl.ds(0, 256), deep]),
            (stage.at[one], weights.at[kind, core, pl.ds(256, 128), deep]),
        )

    for o in (2, 1, 3):
        for kind, coord, peer in ((0, x, x_peer(o)), (1, y, y_peer(o))):
            for src, dst in pieces(kind, lax.rem(coord + o, 4), 4 - o):
                remote(src, dst, w_send, w_sem.at[kind, 4 - o], peer)
    for kind, coord in ((0, x), (1, y)):
        for src, dst in pieces(kind, coord, 0):
            pltpu.make_async_copy(src, dst, own_sem).start()
            remote(src, dst, pass_send, pass_sem, sibling)

    tail_pair.wait_recv()
    tail[2] = tail[0] + tail[1]
    tail_all = remote(tail.at[2], tail.at[3], tail_send.at[1], tail_sem.at[1], z_peer)

    rows_copy.wait_recv()
    pl.semaphore_wait(ping_sem, 2)
    for o in (2, 1, 3):
        remote(rows_in, rows.at[4 - o], ring_send, ring_sem, x_peer(o))
        remote(rows_in, rows.at[8 - o], ring_send, ring_sem, y_peer(o))
    rows_own = rows_in[...].reshape(128, 128)
    tail_all.wait_recv()
    tail_columns = jnp.concatenate([tail[2] + tail[3], jnp.zeros((112, 128), BF16)], axis=0)
    across = (((1,), (1,)), ((), ()))
    tail_part = lax.dot_general(rows_own, tail_columns, across, preferred_element_type=F32)

    for slot in (3, 1, 2):
        for kind in range(2):
            block = weights.at[kind, core, :, pl.ds(slot * 128, 128)]
            wait_bytes(block, w_sem.at[kind, slot])
            remote(block, block, pass_send, pass_sem, sibling)
    wait_bytes(weights.at[0, 0, :, pl.ds(0, 256)], own_sem)
    wait_bytes(rows.at[pl.ds(0, 6)], ring_sem)
    wait_bytes(weights.at[0], pass_sem)

    def store(j, value):
        for half in range(2):
            for draft in range(2):
                start = half * 1024 + draft * 16 + j
                first = half * 64 + draft * 32
                send_f32[pl.ds(start, 32, stride=32), :] = value[first : first + 32]

    in_low = z_hi == 0
    for index in range(2):
        lhs = jnp.concatenate([rows_own] + [rows[index * 4 + s].reshape(128, 128) for s in (1, 2, 3)], axis=1)
        for side in range(2):
            part = lax.dot_general(lhs, weights[index, side], across, preferred_element_type=F32)
            for t in range(3):
                store(index * 6 + side * 3 + t, part[:, t * 128 : (t + 1) * 128])
            if side == 0:
                low = [split_low(part[:, t * 128 : (t + 1) * 128]) for t in range(2)]
                if index == 0:
                    low_x = low
                else:
                    low_y = low
            elif index == 1:
                low_gates = split_low(part[:, 256:384])
    store(12, jnp.where(in_low, low_x[0], low_gates))
    store(13, jnp.where(in_low, low_x[1], tail_part))
    store(14, jnp.where(in_low, low_y[0], split_low(tail_part)))
    store(15, low_y[1])
    for block in range(8):
        send[pl.ds(block * 8, 8)] = send_f32[pl.ds(block * 256, 256), :].astype(BF16).reshape(8, 32, 128)

    me = z_hi * 32 + loop_id

    def send_sums(i, _):
        owner = lax.rem(me + i, 64)
        pltpu.make_async_remote_copy(
            src_ref=send.at[owner], dst_ref=received.at[me], send_sem=sums_send, recv_sem=sums_recv,
            device_id=(lax.rem(owner, 32), lax.div(owner, 32) * 2 + core), device_id_type=MESH,
        ).start()
        return 0

    lax.fori_loop(1, 64, send_sums, 0)
    keep = pltpu.make_async_copy(send.at[me], received.at[me], own_sem)
    keep.start()

    for load in loads[2:]:
        load.wait()
    keep.wait()
    wait_bytes(received.at[pl.ds(0, 63)], sums_recv)

    tails = None
    for half in range(2):
        for holder in range(4):
            sum_x = sum_y = None
            for lo in range(2):
                for k in range(4):
                    one_x = received[half * 32 + lo * 16 + k * 4 + holder].astype(F32)
                    one_y = received[half * 32 + lo * 16 + holder * 4 + k].astype(F32)
                    sum_x = one_x if sum_x is None else sum_x + one_x
                    sum_y = one_y if sum_y is None else sum_y + one_y
            if half == 1:
                tails = sum_x if tails is None else tails + sum_x
            for draft in range(2):
                b = draft * 16
                for index, total in enumerate((sum_x, sum_y)):
                    for side in range(2):
                        j = b + index * 6 + side * 3
                        pair, last = total[j : j + 2], total[j + 2 : j + 3]
                        if half == 0 and side == 0:
                            pair = pair + total[b + 12 + index * 2 : b + 14 + index * 2]
                        if half == 1 and side == 1 and index == 1 and holder == 3:
                            last = last + total[b + 12 : b + 13]
                        base = half * 48 + side * 24
                        tiles[draft, pl.ds(base + index * 8 + 2 * holder, 2), :] = pair
                        tiles[draft, pl.ds(base + 16 + index * 4 + holder, 1), :] = last

    lane = lax.broadcasted_iota(jnp.int32, (24, 128), 1)
    row = lax.broadcasted_iota(jnp.int32, (24, 128), 0)
    gate_rows = []
    for draft in range(2):
        tail_row = tails[draft * 16 + 13 : draft * 16 + 14] + tails[draft * 16 + 14 : draft * 16 + 15]
        for grp in range(4):
            block = tiles[draft, pl.ds(grp * 24, 24), :]
            if grp:
                block = pltpu.roll(block, 4 * grp, 1)
            rolled[draft, pl.ds(grp * 24 + 1, 24), :] = block
            if grp:
                before = rolled[draft, pl.ds(grp * 24, 24), :]
                merged = jnp.where(lane >= 4 * grp, block, before)
                edge = (row == 0) & (lane >= 4 * grp - 4) & (lane < 4 * grp)
                block_out = jnp.where(edge, jnp.broadcast_to(tail_row, (24, 128)), merged)
            else:
                block_out = block
            flat[draft, pl.ds(grp * 24, 24), :] = block_out
        last = rolled[draft, pl.ds(96, 1), :]
        gate_rows.append(jnp.where(lane[0:1] >= 12, tail_row, last))

    queries_t = jnp.concatenate([flat[0, 0:16, :], flat[1, 0:16, :]], axis=0).T
    for head in range(8):
        totals = [jnp.zeros((8, 512), F32), jnp.zeros((8, 512), F32)]
        for part in range(8):
            block = memory[head, pl.ds(part * 32, 32), :]
            k = (part % 4) * 32
            for draft in range(2):
                at = draft * 16 + head * 2 + part // 4
                product = queries_t[k : k + 32, at : at + 1] * block
                totals[draft] = totals[draft] + jnp.sum(product.reshape(4, 8, 512), axis=0)
        for draft in range(2):
            numer[draft, pl.ds(head, 1), :] = jnp.sum(totals[draft], axis=0, keepdims=True)

    def by_head(draft, first, width):
        return [flat[draft, pl.ds(first + i, 8, stride=width), :] for i in range(width)]

    def dot(a, b):
        total = a[0] * b[0]
        for i in range(1, len(a)):
            total = total + a[i] * b[i]
        return jnp.sum(total, axis=1, keepdims=True)

    q = [by_head(d, 0, 2) for d in range(2)]
    keys = [[k * 0.0625 for k in by_head(d, 16, 2)] for d in range(2)]
    v = [by_head(d, 32, 4) for d in range(2)]
    out_gate = [by_head(d, 64, 4) for d in range(2)]
    n_old = [norm[:, 0:128], norm[:, 128:256]]
    admit_bias = to_column(bias[0:1, :])
    forget_bias = to_column(bias[1:2, :])
    stabilizer = to_column(stab[...])
    forget, admit = [], []
    for draft in range(2):
        admit_pre = to_column(gate_rows[draft]) + admit_bias
        forget_pre = to_column(gate_rows[draft], 8) + forget_bias
        log_forget = jnp.minimum(forget_pre, 0.0) - jnp.log1p(jnp.exp(-jnp.abs(forget_pre)))
        new_stabilizer = jnp.maximum(log_forget + stabilizer, admit_pre)
        forget.append(jnp.exp(log_forget + stabilizer - new_stabilizer))
        admit.append(jnp.exp(admit_pre - new_stabilizer))
        stabilizer = new_stabilizer
    square = (8, 8)
    diagonal = lax.broadcasted_iota(jnp.int32, square, 0) == lax.broadcasted_iota(jnp.int32, square, 1)
    stab_out_ref[...] = jnp.sum(
        jnp.where(diagonal, jnp.broadcast_to(stabilizer, square), 0.0), axis=0, keepdims=True
    )
    f0, f1, a0, a1 = forget[0], forget[1], admit[0], admit[1]
    q0k0, q1k0, q1k1 = dot(q[0], keys[0]), dot(q[1], keys[0]), dot(q[1], keys[1])
    den0 = f0 * dot(q[0], n_old) + a0 * q0k0
    den1 = f1 * (f0 * dot(q[1], n_old) + a0 * q1k0) + a1 * q1k1
    inverse = [1.0 / jnp.maximum(jnp.abs(den0), 1.0), 1.0 / jnp.maximum(jnp.abs(den1), 1.0)]
    for i in range(2):
        norm_out_ref[0, :, pl.ds(i * 128, 128)] = f1 * (f0 * n_old[i] + a0 * keys[0][i]) + a1 * keys[1][i]

    messages = []
    for draft in range(2):
        hidden = []
        for j in range(4):
            old = numer[draft, :, pl.ds(j * 128, 128)]
            if draft == 0:
                top = f0 * old + (a0 * q0k0) * v[0][j]
            else:
                top = f1 * (f0 * old + (a0 * q1k0) * v[0][j]) + (a1 * q1k1) * v[1][j]
            hidden.append(top * inverse[draft])
        square_sum = hidden[0] * hidden[0]
        for j in range(1, 4):
            square_sum = square_sum + hidden[j] * hidden[j]
        mean = jnp.sum(jnp.sum(square_sum, axis=1, keepdims=True), axis=0, keepdims=True) * (1.0 / 4096.0)
        rescale = lax.rsqrt(mean + 1e-06)
        for j in range(4):
            gain_j = gain[pl.ds(j, 8, stride=4), :]
            messages.append(hidden[j] * rescale * gain_j * jax.nn.sigmoid(out_gate[draft][j]))
    readout[...] = jnp.concatenate(messages, axis=0).astype(BF16)

    def send_readout(i, _):
        to = lax.rem(loop_id + i, 32)
        pltpu.make_async_remote_copy(
            src_ref=readout, dst_ref=gathered.at[loop_id], send_sem=gather_send, recv_sem=gather_recv,
            device_id=(to, grp_id), device_id_type=MESH,
        ).start()
        return 0

    lax.fori_loop(1, 32, send_readout, 0)
    keep = pltpu.make_async_copy(readout, gathered.at[loop_id], own_sem)
    keep.start()

    for j in range(4):
        scaled[0, :, pl.ds(j * 128, 128)] = (f1 * a0) * v[0][j]
        scaled[1, :, pl.ds(j * 128, 128)] = a1 * v[1][j]
    keys_t = (jnp.concatenate([flat[0, 16:32, :], flat[1, 16:32, :]], axis=0) * 0.0625).T
    kept = f1 * f0
    for head in range(8):
        fade = jnp.broadcast_to(kept[head : head + 1, :], (32, 512))
        row0, row1 = scaled[0, pl.ds(head, 1), :], scaled[1, pl.ds(head, 1), :]
        for part in range(8):
            k = (part % 4) * 32
            at = head * 2 + part // 4
            k0 = keys_t[k : k + 32, at : at + 1]
            k1 = keys_t[k : k + 32, 16 + at : 17 + at]
            old = memory[head, pl.ds(part * 32, 32), :]
            memory_out_ref[0, head, pl.ds(part * 32, 32), :] = fade * old + k0 * row0 + k1 * row1

    keep.wait()
    wait_bytes(gathered.at[pl.ds(0, 31)], gather_recv)

    for block in range(8):
        gathered_f32[pl.ds(block * 256, 256), :] = gathered[pl.ds(block * 4, 4)].reshape(256, 128).astype(F32)
    for draft in range(2):
        for j in range(4):
            for head in range(8):
                piece = gathered_f32[pl.ds(draft * 32 + j * 8 + head, 32, stride=64), :]
                left[pl.ds(draft * 32, 32), pl.ds((head * 4 + j) * 128, 128)] = piece.astype(BF16)
    product = jnp.dot(left[...], out_weight[...], preferred_element_type=F32)
    mixed_ref[...] = product.astype(BF16).reshape(2, 32, 128)

    rows_copy.wait_send()
    tail_pair.wait_send()
    tail_all.wait_send()
    wait_bytes(weights.at[0, :, :, pl.ds(0, 384)], w_send)
    wait_bytes(weights.at[0], pass_send)
    wait_bytes(rows.at[pl.ds(0, 6)], ring_send)
    wait_bytes(send.at[pl.ds(0, 63)], sums_send)
    wait_bytes(gathered.at[pl.ds(0, 31)], gather_send)


def body(inputs, in_weight, gate_bias, memory, normalizer, stabilizer, out_gain, out_weight):
    vmem = pl.BlockSpec(memory_space=pltpu.VMEM)
    hbm = pl.BlockSpec(memory_space=pltpu.HBM)
    dma = pltpu.SemaphoreType.DMA
    out_shape = (
        jax.ShapeDtypeStruct((2, 32, 128), BF16),
        jax.ShapeDtypeStruct(memory.shape, F32),
        jax.ShapeDtypeStruct((1, 8, 256), F32),
        jax.ShapeDtypeStruct((1, 8), F32),
    )
    return pl.pallas_call(
        exchange_kernel,
        out_shape=out_shape,
        in_specs=[hbm] * 8,
        out_specs=(vmem,) * 4,
        scratch_shapes=[
            pltpu.VMEM((3076, 128), BF16),
            pltpu.VMEM((8, 256, 512), F32),
            pltpu.VMEM((4096, 128), BF16),
            pltpu.VMEM((2, 8), F32),
            pltpu.VMEM((8, 256), F32),
            pltpu.VMEM((1, 8), F32),
            pltpu.VMEM((32, 128), F32),
            pltpu.VMEM((2, 2, 32, 128), BF16),
            pltpu.VMEM((8, 2, 2, 32, 128), BF16),
            pltpu.VMEM((4, 16, 128), BF16),
            pltpu.VMEM((16, 128), F32),
            pltpu.VMEM((2, 2, 384, 512), BF16),
            pltpu.VMEM((2048, 128), F32),
            pltpu.VMEM((64, 32, 128), BF16),
            pltpu.VMEM((64, 32, 128), BF16),
            pltpu.VMEM((2, 96, 128), F32),
            pltpu.VMEM((2, 104, 128), F32),
            pltpu.VMEM((2, 96, 128), F32),
            pltpu.VMEM((2, 8, 512), F32),
            pltpu.VMEM((2, 8, 512), F32),
            pltpu.VMEM((64, 128), BF16),
            pltpu.VMEM((32, 64, 128), BF16),
            pltpu.VMEM((2048, 128), F32),
            pltpu.VMEM((64, 4096), BF16),
            dma((8,)),
            dma,
            dma,
            dma,
            dma,
            dma,
            dma((2,)),
            dma((2,)),
            dma,
            dma((2, 4)),
            dma,
            dma,
            dma,
            dma,
            dma,
            dma,
            pltpu.SemaphoreType.REGULAR,
        ],
        compiler_params=pltpu.CompilerParams(
            collective_id=0, has_side_effects=True, vmem_limit_bytes=40 * 2**20
        ),
    )(*(
        pltpu.with_memory_space_constraint(operand, pltpu.HBM)
        for operand in (
            inputs, in_weight.T, gate_bias, memory, normalizer, stabilizer, out_gain.reshape(32, 128), out_weight
        )
    ))


def solution(mesh):
    in_specs = (
        P(None, "grp", "loop"),
        P("loop", "grp"),
        P(),
        P(("grp", "loop"), None, None, None),
        P(("grp", "loop"), None, None),
        P(("grp", "loop"), None),
        P(),
        P(None, "loop"),
    )
    out_specs = (
        P(None, "grp", "loop"),
        P(("grp", "loop"), None, None, None),
        P(("grp", "loop"), None, None),
        P(("grp", "loop"), None),
    )
    return jax.shard_map(body, mesh=mesh, in_specs=in_specs, out_specs=out_specs, check_vma=False)
```

time: 863 us -> 41.6 us (0.05); the launches traced: 847 us -> 41.4 us
  waiting for transfers between devices: 579 us -> 0 us
  blocking collectives: 163 us -> 0 us
  starting transfers between devices: 51 us -> 0 us
  Pallas kernels: 0 us -> 37 us
  between operations: 14.1 us -> 0.64 us
  other arithmetic: 12.3 us -> 0 us
  local copies, waits for them, and re-layouts: 15.7 us -> 3.73 us
  matrix products: 10.2 us -> 0 us
    while x4 -> x0, waiting for transfers between devices: 569 us -> none
    all_gather x4 -> x0, blocking collectives: 163 us -> none  [the longest x2 133 us: stepper(): lax.all_gather(readout[None], 'loop', axis=1, tiled=True)]
    all_to_all x2 -> x0, starting transfers between devices: 50.9 us -> none  [stepper(): lax.all_to_all(owned_step, 'grp', split_axis=1, concat_axis=3, tiled=True)]
    pallas_call x0 -> x1, Pallas kernels: none -> 37 us  [body(): pl.pallas_call(exchange_kernel, out_shape=out_shape, in_specs=[hbm] * 8,...]
    dot_general x6 -> x0, matrix products: 10.2 us -> none  [the longest x2 8.53 us: advance(): jnp.einsum('rhk,rhkv->rhv', queries, memory, precision=lax.Precision.HIGH...]
    add x2 -> x0, other arithmetic: 9.57 us -> none  [advance(): forget[..., None, None] * memory]
    all_to_all x2 -> x0, waiting for transfers between devices: 9.45 us -> none  [stepper(): lax.all_to_all(owned_step, 'grp', split_axis=1, concat_axis=3, tiled=True)]
  transfers between devices with their start and end apart: 4 -> 0, of which waited for: 4 -> 0; matrix products, arithmetic and copies ran while one was open for 0% -> 0% of each run, Pallas kernels for 0% -> 0%
where the time goes in v1:
time: 41.6 us; the launch traced here: 41.4 us
  Pallas kernels  37 us (89%)
  local copies, waits for them, and re-layouts  3.73 us (9%)
  between operations  0.64 us (2%)
    pallas_call x1, Pallas kernels, body(): pl.pallas_call(exchange_kernel, out_shape=out_shape, in_specs=[hbm] * 8,...  37 us
    unnamed x4, local copies, waits for them, and re-layouts  3.73 us

profile of v1, /device:TPU:1, one launch (start us, length us, event | category | flops | bytes accessed | tf_op | source)
XLA Modules:
  0.0 41.4 jit_solution(3804438585123695730)
XLA Ops:
  0.6 37.0 %shard_map.111 = (bf16[2,32,128]{2,1,0:T(8,128)(2,1)S(1)}, f32[1,8,256,512]{3,2,1,0:T(8,128)S(1)}, f32[1,8,256]{2,1,0:T(8,128)S(1)}, f32[1,8]{1,0:T(1,128)S(1)}) custom-call(bf16[2,32,128]{2,1,0:T(8,128)(2,1)} %inputs_hbm.1, bf16[3076,128]{1,0:T(8,128)(2,1)} %bitcast.2, f32[2,8]{1,0:T(2,128)} %bias_hbm.1, f32[1,8,256,512]{3,2,1,0:T(8,128)} %memory_hbm.1, ...), custom_call_target="tpu_custom_call" | custom-call | tf_op jit(solution)/shard_map/pallas_call | solution.py:366
  37.7 0.6 %copy.16 = bf16[2,32,128]{2,1,0:T(8,128)(2,1)} copy(bf16[2,32,128]{2,1,0:T(8,128)(2,1)S(1)} %get-tuple-element.8) | data formatting | bytes 32768
  38.3 2.0 %copy.17 = f32[1,8,256,512]{3,2,1,0:T(8,128)} copy(f32[1,8,256,512]{3,2,1,0:T(8,128)S(1)} %get-tuple-element.9) | data formatting | bytes 8388608
  40.3 0.6 %copy.18 = f32[1,8,256]{2,1,0:T(8,128)} copy(f32[1,8,256]{2,1,0:T(8,128)S(1)} %get-tuple-element.10) | data formatting | bytes 16384
  40.9 0.5 %copy.19 = f32[1,8]{1,0:T(1,128)} copy(f32[1,8]{1,0:T(1,128)S(1)} %get-tuple-element.11) | data formatting | bytes 64

commit v2 on v1

v2 whole, which is shorter than its diff:
```python
import jax
import jax.numpy as jnp
from jax import lax
from jax.experimental import pallas as pl
from jax.experimental.pallas import tpu as pltpu
from jax.sharding import PartitionSpec as P

MESH = pl.DeviceIdType.MESH
F32 = jnp.float32
BF16 = jnp.bfloat16


def split_low(value):
    return value - value.astype(BF16).astype(F32)


def offsets(deep):
    steps = [(o_z, o_y, o_x) for o_z in range(deep) for o_y in range(4) for o_x in range(4)]
    return sorted(steps[1:], key=lambda step: -sum(min(o, 4 - o) for o in step))


def to_column(row, shift=0):
    wide = jnp.broadcast_to(row, (8, row.shape[1]))
    lane = lax.broadcasted_iota(jnp.int32, wide.shape, 1)
    head = lax.broadcasted_iota(jnp.int32, wide.shape, 0)
    return jnp.sum(jnp.where(lane == head + shift, wide, 0.0), axis=1, keepdims=True)


def exchange_kernel(
    inputs_hbm, weight_hbm, bias_hbm, memory_hbm, norm_hbm, stab_hbm, gain_hbm, out_weight_hbm,
    mixed_ref, memory_out_ref, norm_out_ref, stab_out_ref,
    stage, memory, out_weight, bias, norm, stab, gain, rows_in, rows, tail, tail_f32, weights,
    send_f32, send, received, tiles, rolled, flat, numer, scaled, readout, gathered, gathered_f32, left,
    load_sem, own_sem, rows_send, rows_sem, ring_send, ring_sem, tail_send, tail_sem, w_send, w_sem, pass_send,
    pass_sem, sums_send, sums_recv, gather_send, gather_recv, ping_sem,
):
    loop_id = lax.axis_index("loop")
    grp_id = lax.axis_index("grp")
    x = lax.rem(loop_id, 4)
    y = lax.rem(lax.div(loop_id, 4), 4)
    z_lo = lax.div(loop_id, 16)
    z_hi = lax.div(grp_id, 2)
    core = lax.rem(grp_id, 2)

    def x_peer(o):
        return (z_lo * 16 + y * 4 + lax.rem(x + o, 4), grp_id)

    def y_peer(o):
        return (z_lo * 16 + lax.rem(y + o, 4) * 4 + x, grp_id)

    z_peer = (loop_id, (1 - z_hi) * 2 + core)
    other_lo = (1 - z_lo) * 16 + y * 4 + x
    z_near = [(other_lo, grp_id), (other_lo, (1 - z_hi) * 2 + core)]
    sibling = (loop_id, z_hi * 2 + 1 - core)

    loads = [
        pltpu.make_async_copy(src, dst, load_sem.at[i])
        for i, (src, dst) in enumerate((
            (inputs_hbm, rows_in.at[z_hi]),
            (weight_hbm, stage),
            (bias_hbm, bias),
            (stab_hbm, stab),
            (norm_hbm.at[0], norm),
            (gain_hbm, gain),
            (memory_hbm.at[0], memory),
            (out_weight_hbm, out_weight),
        ))
    ]
    for load in loads:
        load.start()

    barrier = pltpu.get_barrier_semaphore()
    peers = [x_peer(2), y_peer(2), z_peer] + z_near
    peers += [x_peer(1), x_peer(3), y_peer(1), y_peer(3), sibling]
    for peer in peers:
        pl.semaphore_signal(barrier, inc=1, device_id=peer, device_id_type=MESH)

    loads[0].wait()
    loads[1].wait()
    tail_f32[...] = jnp.zeros_like(tail_f32)
    tail_f32[0:4, :] = stage[3072:3076, :].astype(F32)
    tail[0] = pltpu.roll(tail_f32[...], grp_id * 4, 0).astype(BF16)

    pl.semaphore_wait(barrier, len(peers))

    def remote(src, dst, send_sem, recv_sem, peer):
        copy = pltpu.make_async_remote_copy(
            src_ref=src, dst_ref=dst, send_sem=send_sem, recv_sem=recv_sem, device_id=peer, device_id_type=MESH
        )
        copy.start()
        return copy

    def wait_bytes(ref, sem):
        pltpu.make_async_copy(ref, ref, sem).wait()

    rows_copy = remote(rows_in.at[z_hi], rows_in.at[z_hi], rows_send, rows_sem, z_peer)
    for peer in z_near:
        pl.semaphore_signal(ping_sem, inc=1, device_id=peer, device_id_type=MESH)
    tail_pair = remote(tail.at[0], tail.at[1], tail_send.at[0], tail_sem.at[0], sibling)

    def pieces(kind, holder, slot):
        wide = pl.ds(pl.multiple_of(kind * 1024 + holder * 256, 128), 256)
        one = pl.ds(pl.multiple_of(2048 + kind * 512 + holder * 128, 128), 128)
        deep = pl.ds(slot * 128, 128)
        return (
            (stage.at[wide], weights.at[kind, core, pl.ds(0, 256), deep]),
            (stage.at[one], weights.at[kind, core, pl.ds(256, 128), deep]),
        )

    for o in (2, 1, 3):
        for kind, coord, peer in ((0, x, x_peer(o)), (1, y, y_peer(o))):
            for src, dst in pieces(kind, lax.rem(coord + o, 4), 4 - o):
                remote(src, dst, w_send, w_sem.at[kind, 4 - o], peer)
    for kind, coord in ((0, x), (1, y)):
        for src, dst in pieces(kind, coord, 0):
            pltpu.make_async_copy(src, dst, own_sem).start()
            remote(src, dst, pass_send, pass_sem, sibling)

    tail_pair.wait_recv()
    tail[2] = tail[0] + tail[1]
    tail_all = remote(tail.at[2], tail.at[3], tail_send.at[1], tail_sem.at[1], z_peer)

    rows_copy.wait_recv()
    pl.semaphore_wait(ping_sem, 2)
    for o in (2, 1, 3):
        remote(rows_in, rows.at[4 - o], ring_send, ring_sem, x_peer(o))
        remote(rows_in, rows.at[8 - o], ring_send, ring_sem, y_peer(o))
    rows_own = rows_in[...].reshape(128, 128)
    tail_all.wait_recv()
    tail_columns = jnp.concatenate([tail[2] + tail[3], jnp.zeros((112, 128), BF16)], axis=0)
    across = (((1,), (1,)), ((), ()))
    tail_part = lax.dot_general(rows_own, tail_columns, across, preferred_element_type=F32)

    for slot in (3, 1, 2):
        for kind in range(2):
            block = weights.at[kind, core, :, pl.ds(slot * 128, 128)]
            wait_bytes(block, w_sem.at[kind, slot])
            remote(block, block, pass_send, pass_sem, sibling)
    wait_bytes(weights.at[0, 0, :, pl.ds(0, 256)], own_sem)
    wait_bytes(rows.at[pl.ds(0, 6)], ring_sem)
    wait_bytes(weights.at[0], pass_sem)

    parts = [
        [
            lax.dot_general(lhs, weights[kind, side], across, preferred_element_type=F32)
            for side in range(2)
        ]
        for kind in range(2)
        for lhs in [jnp.concatenate([rows_own] + [rows[kind * 4 + s].reshape(128, 128) for s in (1, 2, 3)], axis=1)]
    ]
    columns = [
        parts[kind][side][:, t * 128 : (t + 1) * 128] for kind in range(2) for side in range(2) for t in range(3)
    ]
    in_low = z_hi == 0
    columns += [
        jnp.where(in_low, split_low(columns[0]), split_low(columns[11])),
        jnp.where(in_low, split_low(columns[1]), tail_part),
        jnp.where(in_low, split_low(columns[6]), split_low(tail_part)),
        split_low(columns[7]),
    ]
    me = z_hi * 32 + loop_id
    for draft in range(2):
        for j, value in enumerate(columns):
            for half in range(2):
                first = half * 64 + draft * 32
                send_f32[pl.ds(half * 512 + j, 32, stride=16), :] = value[first : first + 32]
        for block in range(4):
            packed = send_f32[pl.ds(block * 256, 256), :].astype(BF16)
            send[draft, pl.ds(block * 16, 16)] = packed.reshape(16, 16, 128)
        for o_z, o_y, o_x in offsets(4):
            to = lax.rem(z_lo * 16 + z_hi * 32 + o_z * 16, 64) + lax.rem(y + o_y, 4) * 4 + lax.rem(x + o_x, 4)
            pltpu.make_async_remote_copy(
                src_ref=send.at[draft, to], dst_ref=received.at[draft, me],
                send_sem=sums_send.at[draft], recv_sem=sums_recv.at[draft],
                device_id=(lax.rem(to, 32), lax.div(to, 32) * 2 + core), device_id_type=MESH,
            ).start()
    keep = pltpu.make_async_copy(send.at[:, me], received.at[:, me], own_sem)
    keep.start()

    for load in loads[2:]:
        load.wait()
    keep.wait()

    n_old = [norm[:, 0:128], norm[:, 128:256]]
    admit_bias = to_column(bias[0:1, :])
    forget_bias = to_column(bias[1:2, :])
    stabilizer = to_column(stab[...])
    q, keys, v, out_gate, forget, admit = [], [], [], [], [], []
    lane = lax.broadcasted_iota(jnp.int32, (24, 128), 1)
    row = lax.broadcasted_iota(jnp.int32, (24, 128), 0)

    def by_head(draft, first, width):
        return [flat[draft, pl.ds(first + i, 8, stride=width), :] for i in range(width)]

    def dot(a, b):
        total = a[0] * b[0]
        for i in range(1, len(a)):
            total = total + a[i] * b[i]
        return jnp.sum(total, axis=1, keepdims=True)

    for draft in range(2):
        wait_bytes(received.at[draft, pl.ds(0, 63)], sums_recv.at[draft])

        tails = None
        for half in range(2):
            for holder in range(4):
                sum_x = sum_y = None
                for lo in range(2):
                    for k in range(4):
                        one_x = received[draft, half * 32 + lo * 16 + k * 4 + holder].astype(F32)
                        one_y = received[draft, half * 32 + lo * 16 + holder * 4 + k].astype(F32)
                        sum_x = one_x if sum_x is None else sum_x + one_x
                        sum_y = one_y if sum_y is None else sum_y + one_y
                if half == 1:
                    tails = sum_x if tails is None else tails + sum_x
                for kind, total in enumerate((sum_x, sum_y)):
                    for side in range(2):
                        j = kind * 6 + side * 3
                        pair, last = total[j : j + 2], total[j + 2 : j + 3]
                        if half == 0 and side == 0:
                            pair = pair + total[12 + kind * 2 : 14 + kind * 2]
                        if half == 1 and side == 1 and kind == 1 and holder == 3:
                            last = last + total[12:13]
                        base = half * 48 + side * 24
                        tiles[pl.ds(base + kind * 8 + 2 * holder, 2), :] = pair
                        tiles[pl.ds(base + 16 + kind * 4 + holder, 1), :] = last

        tail_row = tails[13:14] + tails[14:15]
        for grp in range(4):
            block = tiles[pl.ds(grp * 24, 24), :]
            if grp:
                block = pltpu.roll(block, 4 * grp, 1)
            rolled[pl.ds(grp * 24 + 1, 24), :] = block
            if grp:
                before = rolled[pl.ds(grp * 24, 24), :]
                merged = jnp.where(lane >= 4 * grp, block, before)
                edge = (row == 0) & (lane >= 4 * grp - 4) & (lane < 4 * grp)
                block = jnp.where(edge, jnp.broadcast_to(tail_row, (24, 128)), merged)
            flat[draft, pl.ds(grp * 24, 24), :] = block
        gates = jnp.where(lane[0:1] >= 12, tail_row, rolled[pl.ds(96, 1), :])

        queries_t = flat[draft, 0:16, :].T
        for head in range(8):
            total = jnp.zeros((8, 512), F32)
            for part in range(8):
                block = memory[head, pl.ds(part * 32, 32), :]
                k = (part % 4) * 32
                at = head * 2 + part // 4
                product = queries_t[k : k + 32, at : at + 1] * block
                total = total + jnp.sum(product.reshape(4, 8, 512), axis=0)
            numer[pl.ds(head, 1), :] = jnp.sum(total, axis=0, keepdims=True)

        q.append(by_head(draft, 0, 2))
        keys.append([k * 0.0625 for k in by_head(draft, 16, 2)])
        v.append(by_head(draft, 32, 4))
        out_gate = by_head(draft, 64, 4)
        admit_pre = to_column(gates) + admit_bias
        forget_pre = to_column(gates, 8) + forget_bias
        log_forget = jnp.minimum(forget_pre, 0.0) - jnp.log1p(jnp.exp(-jnp.abs(forget_pre)))
        new_stabilizer = jnp.maximum(log_forget + stabilizer, admit_pre)
        forget.append(jnp.exp(log_forget + stabilizer - new_stabilizer))
        admit.append(jnp.exp(admit_pre - new_stabilizer))
        stabilizer = new_stabilizer

        on_old = forget[0] if draft == 0 else forget[0] * forget[1]
        on_keys = [admit[0]] if draft == 0 else [forget[1] * admit[0], admit[1]]
        on_values = [on_keys[i] * dot(q[draft], keys[i]) for i in range(draft + 1)]
        below = on_old * dot(q[draft], n_old)
        for part in on_values:
            below = below + part
        inverse = 1.0 / jnp.maximum(jnp.abs(below), 1.0)
        hidden = []
        for j in range(4):
            top = on_old * numer[:, pl.ds(j * 128, 128)]
            for i in range(draft + 1):
                top = top + on_values[i] * v[i][j]
            hidden.append(top * inverse)
        square_sum = hidden[0] * hidden[0]
        for j in range(1, 4):
            square_sum = square_sum + hidden[j] * hidden[j]
        mean = jnp.sum(jnp.sum(square_sum, axis=1, keepdims=True), axis=0, keepdims=True) * (1.0 / 4096.0)
        rescale = lax.rsqrt(mean + 1e-06)
        message = [
            hidden[j] * rescale * gain[pl.ds(j, 8, stride=4), :] * jax.nn.sigmoid(out_gate[j]) for j in range(4)
        ]
        readout[draft] = jnp.concatenate(message, axis=0).astype(BF16)
        for o_z, o_y, o_x in offsets(2):
            to = lax.rem(z_lo + o_z, 2) * 16 + lax.rem(y + o_y, 4) * 4 + lax.rem(x + o_x, 4)
            pltpu.make_async_remote_copy(
                src_ref=readout.at[draft], dst_ref=gathered.at[draft, loop_id],
                send_sem=gather_send.at[draft], recv_sem=gather_recv.at[draft],
                device_id=(to, grp_id), device_id_type=MESH,
            ).start()

    keep = pltpu.make_async_copy(readout, gathered.at[:, loop_id], own_sem)
    keep.start()

    for i in range(2):
        norm_out_ref[0, :, pl.ds(i * 128, 128)] = on_old * n_old[i] + on_keys[0] * keys[0][i] + on_keys[1] * keys[1][i]
    square = (8, 8)
    diagonal = lax.broadcasted_iota(jnp.int32, square, 0) == lax.broadcasted_iota(jnp.int32, square, 1)
    stab_out_ref[...] = jnp.sum(
        jnp.where(diagonal, jnp.broadcast_to(stabilizer, square), 0.0), axis=0, keepdims=True
    )

    for i in range(2):
        for j in range(4):
            scaled[i, :, pl.ds(j * 128, 128)] = on_keys[i] * v[i][j]
    keys_t = (jnp.concatenate([flat[0, 16:32, :], flat[1, 16:32, :]], axis=0) * 0.0625).T
    for head in range(8):
        fade = jnp.broadcast_to(on_old[head : head + 1, :], (32, 512))
        row0, row1 = scaled[0, pl.ds(head, 1), :], scaled[1, pl.ds(head, 1), :]
        for part in range(8):
            k = (part % 4) * 32
            at = head * 2 + part // 4
            k0 = keys_t[k : k + 32, at : at + 1]
            k1 = keys_t[k : k + 32, 16 + at : 17 + at]
            old = memory[head, pl.ds(part * 32, 32), :]
            memory_out_ref[0, head, pl.ds(part * 32, 32), :] = fade * old + k0 * row0 + k1 * row1

    keep.wait()
    for draft in range(2):
        wait_bytes(gathered.at[draft, pl.ds(0, 31)], gather_recv.at[draft])
        for block in range(4):
            piece = gathered[draft, pl.ds(block * 8, 8)].reshape(256, 128)
            gathered_f32[pl.ds(block * 256, 256), :] = piece.astype(F32)
        for j in range(4):
            for head in range(8):
                piece = gathered_f32[pl.ds(j * 8 + head, 32, stride=32), :]
                left[:, pl.ds((head * 4 + j) * 128, 128)] = piece.astype(BF16)
        product = jnp.dot(left[...], out_weight[...], preferred_element_type=F32)
        mixed_ref[draft] = product.astype(BF16)

    rows_copy.wait_send()
    tail_pair.wait_send()
    tail_all.wait_send()
    wait_bytes(weights.at[0, :, :, pl.ds(0, 384)], w_send)
    wait_bytes(weights.at[0], pass_send)
    wait_bytes(rows.at[pl.ds(0, 6)], ring_send)
    for draft in range(2):
        wait_bytes(send.at[draft, pl.ds(0, 63)], sums_send.at[draft])
        wait_bytes(gathered.at[draft, pl.ds(0, 31)], gather_send.at[draft])


def body(inputs, in_weight, gate_bias, memory, normalizer, stabilizer, out_gain, out_weight):
    vmem = pl.BlockSpec(memory_space=pltpu.VMEM)
    hbm = pl.BlockSpec(memory_space=pltpu.HBM)
    dma = pltpu.SemaphoreType.DMA
    out_shape = (
        jax.ShapeDtypeStruct((2, 32, 128), BF16),
        jax.ShapeDtypeStruct(memory.shape, F32),
        jax.ShapeDtypeStruct((1, 8, 256), F32),
        jax.ShapeDtypeStruct((1, 8), F32),
    )
    return pl.pallas_call(
        exchange_kernel,
        out_shape=out_shape,
        in_specs=[hbm] * 8,
        out_specs=(vmem,) * 4,
        scratch_shapes=[
            pltpu.VMEM((3076, 128), BF16),
            pltpu.VMEM((8, 256, 512), F32),
            pltpu.VMEM((4096, 128), BF16),
            pltpu.VMEM((2, 8), F32),
            pltpu.VMEM((8, 256), F32),
            pltpu.VMEM((1, 8), F32),
            pltpu.VMEM((32, 128), F32),
            pltpu.VMEM((2, 2, 32, 128), BF16),
            pltpu.VMEM((8, 2, 2, 32, 128), BF16),
            pltpu.VMEM((4, 16, 128), BF16),
            pltpu.VMEM((16, 128), F32),
            pltpu.VMEM((2, 2, 384, 512), BF16),
            pltpu.VMEM((1024, 128), F32),
            pltpu.VMEM((2, 64, 16, 128), BF16),
            pltpu.VMEM((2, 64, 16, 128), BF16),
            pltpu.VMEM((96, 128), F32),
            pltpu.VMEM((104, 128), F32),
            pltpu.VMEM((2, 96, 128), F32),
            pltpu.VMEM((8, 512), F32),
            pltpu.VMEM((2, 8, 512), F32),
            pltpu.VMEM((2, 32, 128), BF16),
            pltpu.VMEM((2, 32, 32, 128), BF16),
            pltpu.VMEM((1024, 128), F32),
            pltpu.VMEM((32, 4096), BF16),
            dma((8,)),
            dma,
            dma,
            dma,
            dma,
            dma,
            dma((2,)),
            dma((2,)),
            dma,
            dma((2, 4)),
            dma,
            dma,
            dma((2,)),
            dma((2,)),
            dma((2,)),
            dma((2,)),
            pltpu.SemaphoreType.REGULAR,
        ],
        compiler_params=pltpu.CompilerParams(
            collective_id=0, has_side_effects=True, vmem_limit_bytes=40 * 2**20
        ),
    )(*(
        pltpu.with_memory_space_constraint(operand, pltpu.HBM)
        for operand in (
            inputs, in_weight.T, gate_bias, memory, normalizer, stabilizer, out_gain.reshape(32, 128), out_weight
        )
    ))


def solution(mesh):
    in_specs = (
        P(None, "grp", "loop"),
        P("loop", "grp"),
        P(),
        P(("grp", "loop"), None, None, None),
        P(("grp", "loop"), None, None),
        P(("grp", "loop"), None),
        P(),
        P(None, "loop"),
    )
    out_specs = (
        P(None, "grp", "loop"),
        P(("grp", "loop"), None, None, None),
        P(("grp", "loop"), None, None),
        P(("grp", "loop"), None),
    )
    return jax.shard_map(body, mesh=mesh, in_specs=in_specs, out_specs=out_specs, check_vma=False)
```

time: 41.6 us -> 38.2 us (0.918)
  Pallas kernels: 37 us -> 33.7 us
    pallas_call x1, Pallas kernels: 37 us -> 33.7 us  [body(): pl.pallas_call(exchange_kernel, out_shape=out_shape, in_specs=[hbm] * 8,...]
where the time goes in v2:
time: 38.2 us; the launch traced here: 38 us
  Pallas kernels  33.7 us (88%)
  local copies, waits for them, and re-layouts  3.73 us (10%)
  between operations  0.64 us (2%)
    pallas_call x1, Pallas kernels, body(): pl.pallas_call(exchange_kernel, out_shape=out_shape, in_specs=[hbm] * 8,...  33.7 us
    unnamed x4, local copies, waits for them, and re-layouts  3.73 us

profile of v2, /device:TPU:1, one launch (start us, length us, event | category | flops | bytes accessed | tf_op | source)
XLA Modules:
  0.0 38.0 jit_solution(14838715220627755826)
XLA Ops:
  0.6 33.7 %shard_map.111 = (bf16[2,32,128]{2,1,0:T(8,128)(2,1)S(1)}, f32[1,8,256,512]{3,2,1,0:T(8,128)S(1)}, f32[1,8,256]{2,1,0:T(8,128)S(1)}, f32[1,8]{1,0:T(1,128)S(1)}) custom-call(bf16[2,32,128]{2,1,0:T(8,128)(2,1)} %inputs_hbm.1, bf16[3076,128]{1,0:T(8,128)(2,1)} %bitcast.2, f32[2,8]{1,0:T(2,128)} %bias_hbm.1, f32[1,8,256,512]{3,2,1,0:T(8,128)} %memory_hbm.1, ...), custom_call_target="tpu_custom_call" | custom-call | tf_op jit(solution)/shard_map/pallas_call | solution.py:355
  34.3 0.6 %copy.16 = bf16[2,32,128]{2,1,0:T(8,128)(2,1)} copy(bf16[2,32,128]{2,1,0:T(8,128)(2,1)S(1)} %get-tuple-element.8) | data formatting | bytes 32768
  34.9 2.0 %copy.17 = f32[1,8,256,512]{3,2,1,0:T(8,128)} copy(f32[1,8,256,512]{3,2,1,0:T(8,128)S(1)} %get-tuple-element.9) | data formatting | bytes 8388608
  36.9 0.6 %copy.18 = f32[1,8,256]{2,1,0:T(8,128)} copy(f32[1,8,256]{2,1,0:T(8,128)S(1)} %get-tuple-element.10) | data formatting | bytes 16384
  37.5 0.5 %copy.19 = f32[1,8]{1,0:T(1,128)} copy(f32[1,8]{1,0:T(1,128)S(1)} %get-tuple-element.11) | data formatting | bytes 64

commit v3 on v2

--- a/solution.py
+++ b/solution.py
@@ -342,6 +342,16 @@
         wait_bytes(gathered.at[draft, pl.ds(0, 31)], gather_send.at[draft])
 
 
+def hand_over_kernel(mixed, memory, norm, stab, mixed_out, memory_out, norm_out, stab_out, sem):
+    pairs = [(memory.at[0, head], memory_out.at[0, head]) for head in range(8)]
+    pairs += [(mixed, mixed_out), (norm, norm_out), (stab, stab_out)]
+    copies = [pltpu.make_async_copy(src, dst, sem.at[i]) for i, (src, dst) in enumerate(pairs)]
+    for copy in copies:
+        copy.start()
+    for copy in copies:
+        copy.wait()
+
+
 def body(inputs, in_weight, gate_bias, memory, normalizer, stabilizer, out_gain, out_weight):
     vmem = pl.BlockSpec(memory_space=pltpu.VMEM)
     hbm = pl.BlockSpec(memory_space=pltpu.HBM)
@@ -352,7 +362,7 @@
         jax.ShapeDtypeStruct((1, 8, 256), F32),
         jax.ShapeDtypeStruct((1, 8), F32),
     )
-    return pl.pallas_call(
+    results = pl.pallas_call(
         exchange_kernel,
         out_shape=out_shape,
         in_specs=[hbm] * 8,
@@ -409,6 +419,14 @@
             inputs, in_weight.T, gate_bias, memory, normalizer, stabilizer, out_gain.reshape(32, 128), out_weight
         )
     ))
+    return pl.pallas_call(
+        hand_over_kernel,
+        out_shape=out_shape,
+        in_specs=[vmem] * 4,
+        out_specs=(hbm,) * 4,
+        scratch_shapes=[dma((11,))],
+        compiler_params=pltpu.CompilerParams(vmem_limit_bytes=2 * 2**20),
+    )(*results)
 
 
 def solution(mesh):

time: 38.2 us -> 36.6 us (0.958)
  local copies, waits for them, and re-layouts: 3.73 us -> 0 us
  Pallas kernels: 33.7 us -> 35.8 us
    unnamed x4 -> x0, local copies, waits for them, and re-layouts: 3.73 us -> none
    pallas_call x0 -> x1, Pallas kernels: none -> 2.11 us  [body(): pl.pallas_call(hand_over_kernel, out_shape=out_shape, in_specs=[vmem] * 4...]
where the time goes in v3:
time: 36.6 us; the launch traced here: 36.4 us
  Pallas kernels  35.8 us (98%)
  between operations  0.64 us (2%)
    pallas_call x1, Pallas kernels, body(): pl.pallas_call(exchange_kernel, out_shape=out_shape, in_specs=[hbm] * 8,...  33.7 us
    pallas_call x1, Pallas kernels, body(): pl.pallas_call(hand_over_kernel, out_shape=out_shape, in_specs=[vmem] * 4...  2.11 us

profile of v3, /device:TPU:1, one launch (start us, length us, event | category | flops | bytes accessed | tf_op | source)
XLA Modules:
  0.0 36.4 jit_solution(1423953257269695569)
XLA Ops:
  0.6 33.7 %shard_map.111 = (bf16[2,32,128]{2,1,0:T(8,128)(2,1)S(1)}, f32[1,8,256,512]{3,2,1,0:T(8,128)S(1)}, f32[1,8,256]{2,1,0:T(8,128)S(1)}, f32[1,8]{1,0:T(1,128)S(1)}) custom-call(bf16[2,32,128]{2,1,0:T(8,128)(2,1)} %inputs_hbm.1, bf16[3076,128]{1,0:T(8,128)(2,1)} %bitcast.2, f32[2,8]{1,0:T(2,128)} %bias_hbm.1, f32[1,8,256,512]{3,2,1,0:T(8,128)} %memory_hbm.1, ...), custom_call_target="tpu_custom_call" | custom-call | tf_op jit(solution)/shard_map/pallas_call | solution.py:365
  34.3 2.1 %shard_map.112 = (bf16[2,32,128]{2,1,0:T(8,128)(2,1)}, f32[1,8,256,512]{3,2,1,0:T(8,128)}, f32[1,8,256]{2,1,0:T(8,128)}, f32[1,8]{1,0:T(1,128)}) custom-call(bf16[2,32,128]{2,1,0:T(8,128)(2,1)S(1)} %get-tuple-element.8.mixed, f32[1,8,256,512]{3,2,1,0:T(8,128)S(1)} %get-tuple-element.9.memory, f32[1,8,256]{2,1,0:T(8,128)S(1)} %get-tuple-element.10.norm, ...), custom_call_target="tpu_custom_call" | custom-call | tf_op jit(solution)/shard_map/pallas_call | solution.py:422

commit v4 on v3

--- a/solution.py
+++ b/solution.py
@@ -53,6 +53,12 @@
     z_near = [(other_lo, grp_id), (other_lo, (1 - z_hi) * 2 + core)]
     sibling = (loop_id, z_hi * 2 + 1 - core)
 
+    barrier = pltpu.get_barrier_semaphore()
+    peers = [x_peer(2), y_peer(2), z_peer] + z_near
+    peers += [x_peer(1), x_peer(3), y_peer(1), y_peer(3), sibling]
+    for peer in peers:
+        pl.semaphore_signal(barrier, inc=1, device_id=peer, device_id_type=MESH)
+
     loads = [
         pltpu.make_async_copy(src, dst, load_sem.at[i])
         for i, (src, dst) in enumerate((
@@ -69,12 +75,6 @@
     for load in loads:
         load.start()
 
-    barrier = pltpu.get_barrier_semaphore()
-    peers = [x_peer(2), y_peer(2), z_peer] + z_near
-    peers += [x_peer(1), x_peer(3), y_peer(1), y_peer(3), sibling]
-    for peer in peers:
-        pl.semaphore_signal(barrier, inc=1, device_id=peer, device_id_type=MESH)
-
     loads[0].wait()
     loads[1].wait()
     tail_f32[...] = jnp.zeros_like(tail_f32)
@@ -141,15 +141,12 @@
     wait_bytes(weights.at[0], pass_sem)
 
     parts = [
-        [
-            lax.dot_general(lhs, weights[kind, side], across, preferred_element_type=F32)
-            for side in range(2)
-        ]
+        lax.dot_general(lhs, weights[kind].reshape(768, 512), across, preferred_element_type=F32)
         for kind in range(2)
         for lhs in [jnp.concatenate([rows_own] + [rows[kind * 4 + s].reshape(128, 128) for s in (1, 2, 3)], axis=1)]
     ]
     columns = [
-        parts[kind][side][:, t * 128 : (t + 1) * 128] for kind in range(2) for side in range(2) for t in range(3)
+        parts[kind][:, t * 128 : (t + 1) * 128] for kind in range(2) for t in range(6)
     ]
     in_low = z_hi == 0
     columns += [
@@ -167,13 +164,22 @@
         for block in range(4):
             packed = send_f32[pl.ds(block * 256, 256), :].astype(BF16)
             send[draft, pl.ds(block * 16, 16)] = packed.reshape(16, 16, 128)
-        for o_z, o_y, o_x in offsets(4):
-            to = lax.rem(z_lo * 16 + z_hi * 32 + o_z * 16, 64) + lax.rem(y + o_y, 4) * 4 + lax.rem(x + o_x, 4)
+
+        def send_sums(to):
             pltpu.make_async_remote_copy(
                 src_ref=send.at[draft, to], dst_ref=received.at[draft, me],
                 send_sem=sums_send.at[draft], recv_sem=sums_recv.at[draft],
                 device_id=(lax.rem(to, 32), lax.div(to, 32) * 2 + core), device_id_type=MESH,
             ).start()
+
+        for half in range(2):
+            for o_z, o_y, o_x in offsets(2):
+                send_sums(half * 32 + lax.rem(z_lo + o_z, 2) * 16 + lax.rem(y + o_y, 4) * 4 + lax.rem(x + o_x, 4))
+
+            @pl.when(z_hi != half)
+            def _():
+                send_sums(half * 32 + loop_id)
+
     keep = pltpu.make_async_copy(send.at[:, me], received.at[:, me], own_sem)
     keep.start()
 
@@ -284,13 +290,18 @@
             hidden[j] * rescale * gain[pl.ds(j, 8, stride=4), :] * jax.nn.sigmoid(out_gate[j]) for j in range(4)
         ]
         readout[draft] = jnp.concatenate(message, axis=0).astype(BF16)
-        for o_z, o_y, o_x in offsets(2):
-            to = lax.rem(z_lo + o_z, 2) * 16 + lax.rem(y + o_y, 4) * 4 + lax.rem(x + o_x, 4)
+
+        def send_readout(to):
             pltpu.make_async_remote_copy(
                 src_ref=readout.at[draft], dst_ref=gathered.at[draft, loop_id],
                 send_sem=gather_send.at[draft], recv_sem=gather_recv.at[draft],
                 device_id=(to, grp_id), device_id_type=MESH,
             ).start()
+
+        for to in sorted(range(32), key=lambda d: (min(d % 4, 4 - d % 4) + min(d // 4 % 4, 4 - d // 4 % 4) + d // 16)):
+            @pl.when(loop_id != to)
+            def _():
+                send_readout(to)
 
     keep = pltpu.make_async_copy(readout, gathered.at[:, loop_id], own_sem)
     keep.start()

time: 36.6 us -> 34.9 us (0.954)
  Pallas kernels: 35.8 us -> 34.1 us
    pallas_call x1, Pallas kernels: 33.7 us -> 31.9 us  [body(): pl.pallas_call(exchange_kernel, out_shape=out_shape, in_specs=[hbm] * 8,...]
where the time goes in v4:
time: 34.9 us; the launch traced here: 34.7 us
  Pallas kernels  34.1 us (98%)
  between operations  0.64 us (2%)
    pallas_call x1, Pallas kernels, body(): pl.pallas_call(exchange_kernel, out_shape=out_shape, in_specs=[hbm] * 8,...  31.9 us
    pallas_call x1, Pallas kernels, body(): pl.pallas_call(hand_over_kernel, out_shape=out_shape, in_specs=[vmem] * 4...  2.11 us

profile of v4, /device:TPU:1, one launch (start us, length us, event | category | flops | bytes accessed | tf_op | source)
XLA Modules:
  0.0 34.7 jit_solution(5355820032362558864)
XLA Ops:
  0.6 31.9 %shard_map.111 = (bf16[2,32,128]{2,1,0:T(8,128)(2,1)S(1)}, f32[1,8,256,512]{3,2,1,0:T(8,128)S(1)}, f32[1,8,256]{2,1,0:T(8,128)S(1)}, f32[1,8]{1,0:T(1,128)S(1)}) custom-call(bf16[2,32,128]{2,1,0:T(8,128)(2,1)} %inputs_hbm.1, bf16[3076,128]{1,0:T(8,128)(2,1)} %bitcast.2, f32[2,8]{1,0:T(2,128)} %bias_hbm.1, f32[1,8,256,512]{3,2,1,0:T(8,128)} %memory_hbm.1, ...), custom_call_target="tpu_custom_call" | custom-call | tf_op jit(solution)/shard_map/pallas_call | solution.py:376
  32.6 2.1 %shard_map.112 = (bf16[2,32,128]{2,1,0:T(8,128)(2,1)}, f32[1,8,256,512]{3,2,1,0:T(8,128)}, f32[1,8,256]{2,1,0:T(8,128)}, f32[1,8]{1,0:T(1,128)}) custom-call(bf16[2,32,128]{2,1,0:T(8,128)(2,1)S(1)} %get-tuple-element.8.mixed, f32[1,8,256,512]{3,2,1,0:T(8,128)S(1)} %get-tuple-element.9.memory, f32[1,8,256]{2,1,0:T(8,128)S(1)} %get-tuple-element.10.norm, ...), custom_call_target="tpu_custom_call" | custom-call | tf_op jit(solution)/shard_map/pallas_call | solution.py:433

commit v5 on v4

--- a/solution.py
+++ b/solution.py
@@ -98,23 +98,31 @@
         pl.semaphore_signal(ping_sem, inc=1, device_id=peer, device_id_type=MESH)
     tail_pair = remote(tail.at[0], tail.at[1], tail_send.at[0], tail_sem.at[0], sibling)
 
-    def pieces(kind, holder, slot):
-        wide = pl.ds(pl.multiple_of(kind * 1024 + holder * 256, 128), 256)
-        one = pl.ds(pl.multiple_of(2048 + kind * 512 + holder * 128, 128), 128)
-        deep = pl.ds(slot * 128, 128)
-        return (
-            (stage.at[wide], weights.at[kind, core, pl.ds(0, 256), deep]),
-            (stage.at[one], weights.at[kind, core, pl.ds(256, 128), deep]),
-        )
-
+    def landing(which, kind, slot):
+        tiles_at = pl.ds(0, 256) if which == 0 else pl.ds(256, 128)
+        return weights.at[kind, core, tiles_at, pl.ds(slot * 128, 128)]
+
+    def piece(which, kind, holder):
+        if which == 0:
+            return stage.at[pl.ds(pl.multiple_of(kind * 1024 + holder * 256, 128), 256)]
+        return stage.at[pl.ds(pl.multiple_of(2048 + kind * 512 + holder * 128, 128), 128)]
+
+    def send_pieces(which, steps):
+        for o in steps:
+            for kind, coord, peer in ((0, x, x_peer(o)), (1, y, y_peer(o))):
+                src = piece(which, kind, lax.rem(coord + o, 4))
+                remote(src, landing(which, kind, 4 - o), w_send, w_sem.at[kind, 4 - o, which], peer)
+
+    send_pieces(0, (2, 1, 3))
+    send_pieces(1, (2, 1, 3))
     for o in (2, 1, 3):
-        for kind, coord, peer in ((0, x, x_peer(o)), (1, y, y_peer(o))):
-            for src, dst in pieces(kind, lax.rem(coord + o, 4), 4 - o):
-                remote(src, dst, w_send, w_sem.at[kind, 4 - o], peer)
-    for kind, coord in ((0, x), (1, y)):
-        for src, dst in pieces(kind, coord, 0):
+        remote(rows_in.at[z_hi], rows.at[4 - o, z_hi], ring_send.at[0], ring_sem.at[0], x_peer(o))
+        remote(rows_in.at[z_hi], rows.at[8 - o, z_hi], ring_send.at[0], ring_sem.at[0], y_peer(o))
+    for which in range(2):
+        for kind, coord in ((0, x), (1, y)):
+            src, dst = piece(which, kind, coord), landing(which, kind, 0)
             pltpu.make_async_copy(src, dst, own_sem).start()
-            remote(src, dst, pass_send, pass_sem, sibling)
+            remote(src, dst, pass_send, pass_sem.at[which], sibling)
 
     tail_pair.wait_recv()
     tail[2] = tail[0] + tail[1]
@@ -123,46 +131,61 @@
     rows_copy.wait_recv()
     pl.semaphore_wait(ping_sem, 2)
     for o in (2, 1, 3):
-        remote(rows_in, rows.at[4 - o], ring_send, ring_sem, x_peer(o))
-        remote(rows_in, rows.at[8 - o], ring_send, ring_sem, y_peer(o))
+        remote(rows_in.at[1 - z_hi], rows.at[4 - o, 1 - z_hi], ring_send.at[1], ring_sem.at[1], x_peer(o))
+        remote(rows_in.at[1 - z_hi], rows.at[8 - o, 1 - z_hi], ring_send.at[1], ring_sem.at[1], y_peer(o))
     rows_own = rows_in[...].reshape(128, 128)
+
+    for which in range(2):
+        for slot in (3, 1, 2):
+            for kind in range(2):
+                block = landing(which, kind, slot)
+                wait_bytes(block, w_sem.at[kind, slot, which])
+                remote(block, block, pass_send, pass_sem.at[which], sibling)
     tail_all.wait_recv()
     tail_columns = jnp.concatenate([tail[2] + tail[3], jnp.zeros((112, 128), BF16)], axis=0)
     across = (((1,), (1,)), ((), ()))
     tail_part = lax.dot_general(rows_own, tail_columns, across, preferred_element_type=F32)
-
-    for slot in (3, 1, 2):
-        for kind in range(2):
-            block = weights.at[kind, core, :, pl.ds(slot * 128, 128)]
-            wait_bytes(block, w_sem.at[kind, slot])
-            remote(block, block, pass_send, pass_sem, sibling)
     wait_bytes(weights.at[0, 0, :, pl.ds(0, 256)], own_sem)
-    wait_bytes(rows.at[pl.ds(0, 6)], ring_sem)
-    wait_bytes(weights.at[0], pass_sem)
-
-    parts = [
-        lax.dot_general(lhs, weights[kind].reshape(768, 512), across, preferred_element_type=F32)
-        for kind in range(2)
-        for lhs in [jnp.concatenate([rows_own] + [rows[kind * 4 + s].reshape(128, 128) for s in (1, 2, 3)], axis=1)]
-    ]
-    columns = [
-        parts[kind][:, t * 128 : (t + 1) * 128] for kind in range(2) for t in range(6)
-    ]
+    for half in range(2):
+        wait_bytes(rows.at[pl.ds(0, 3)], ring_sem.at[half])
+
+    def put(j, value):
+        for draft in range(2):
+            for half in range(2):
+                first = half * 64 + draft * 32
+                send_f32[draft, pl.ds(half * 512 + j, 32, stride=16), :] = value[first : first + 32]
+
     in_low = z_hi == 0
-    columns += [
-        jnp.where(in_low, split_low(columns[0]), split_low(columns[11])),
-        jnp.where(in_low, split_low(columns[1]), tail_part),
-        jnp.where(in_low, split_low(columns[6]), split_low(tail_part)),
-        split_low(columns[7]),
-    ]
+    wait_bytes(weights.at[0, :, pl.ds(0, 256)], pass_sem.at[0])
+    lefts, lows = [], []
+    for kind in range(2):
+        lhs = jnp.concatenate([rows_own] + [rows[kind * 4 + s].reshape(128, 128) for s in (1, 2, 3)], axis=1)
+        lefts.append(lhs)
+        part = lax.dot_general(
+            lhs, weights[kind, :, 0:256, :].reshape(512, 512), across, preferred_element_type=F32
+        )
+        for side in range(2):
+            for t in range(2):
+                column = part[:, side * 256 + t * 128 : side * 256 + (t + 1) * 128]
+                put(kind * 6 + side * 3 + t, column)
+                if side == 0:
+                    lows.append(split_low(column))
+    put(13, jnp.where(in_low, lows[1], tail_part))
+    put(14, jnp.where(in_low, lows[2], split_low(tail_part)))
+    put(15, lows[3])
+    wait_bytes(weights.at[0, :, pl.ds(256, 128)], pass_sem.at[1])
+    for kind in range(2):
+        part = lax.dot_general(
+            lefts[kind], weights[kind, :, 256:384, :].reshape(256, 512), across, preferred_element_type=F32
+        )
+        for side in range(2):
+            column = part[:, side * 128 : (side + 1) * 128]
+            put(kind * 6 + side * 3 + 2, column)
+    put(12, jnp.where(in_low, lows[0], split_low(column)))
     me = z_hi * 32 + loop_id
     for draft in range(2):
-        for j, value in enumerate(columns):
-            for half in range(2):
-                first = half * 64 + draft * 32
-                send_f32[pl.ds(half * 512 + j, 32, stride=16), :] = value[first : first + 32]
         for block in range(4):
-            packed = send_f32[pl.ds(block * 256, 256), :].astype(BF16)
+            packed = send_f32[draft, pl.ds(block * 256, 256), :].astype(BF16)
             send[draft, pl.ds(block * 16, 16)] = packed.reshape(16, 16, 128)
 
         def send_sums(to):
@@ -347,7 +370,8 @@
     tail_all.wait_send()
     wait_bytes(weights.at[0, :, :, pl.ds(0, 384)], w_send)
     wait_bytes(weights.at[0], pass_send)
-    wait_bytes(rows.at[pl.ds(0, 6)], ring_send)
+    for half in range(2):
+        wait_bytes(rows.at[pl.ds(0, 3)], ring_send.at[half])
     for draft in range(2):
         wait_bytes(send.at[draft, pl.ds(0, 63)], sums_send.at[draft])
         wait_bytes(gathered.at[draft, pl.ds(0, 31)], gather_send.at[draft])
@@ -391,7 +415,7 @@
             pltpu.VMEM((4, 16, 128), BF16),
             pltpu.VMEM((16, 128), F32),
             pltpu.VMEM((2, 2, 384, 512), BF16),
-            pltpu.VMEM((1024, 128), F32),
+            pltpu.VMEM((2, 1024, 128), F32),
             pltpu.VMEM((2, 64, 16, 128), BF16),
             pltpu.VMEM((2, 64, 16, 128), BF16),
             pltpu.VMEM((96, 128), F32),
@@ -407,14 +431,14 @@
             dma,
             dma,
             dma,
+            dma((2,)),
+            dma((2,)),
+            dma((2,)),
+            dma((2,)),
             dma,
+            dma((2, 4, 2)),
             dma,
             dma((2,)),
-            dma((2,)),
-            dma,
-            dma((2, 4)),
-            dma,
-            dma,
             dma((2,)),
             dma((2,)),
             dma((2,)),

time: 34.9 us -> 34.3 us (0.983)
  Pallas kernels: 34.1 us -> 33.1 us
    pallas_call x1, Pallas kernels: 31.9 us -> 31 us  [body(): pl.pallas_call(exchange_kernel, out_shape=out_shape, in_specs=[hbm] * 8,...]
where the time goes in v5:
time: 34.3 us; the launch traced here: 33.8 us
  Pallas kernels  33.1 us (97%)
  between operations  0.64 us (2%)
    pallas_call x1, Pallas kernels, body(): pl.pallas_call(exchange_kernel, out_shape=out_shape, in_specs=[hbm] * 8,...  31 us
    pallas_call x1, Pallas kernels, body(): pl.pallas_call(hand_over_kernel, out_shape=out_shape, in_specs=[vmem] * 4...  2.11 us

profile of v5, /device:TPU:1, one launch (start us, length us, event | category | flops | bytes accessed | tf_op | source)
XLA Modules:
  0.0 33.8 jit_solution(11140736799420675627)
XLA Ops:
  0.6 31.0 %shard_map.111 = (bf16[2,32,128]{2,1,0:T(8,128)(2,1)S(1)}, f32[1,8,256,512]{3,2,1,0:T(8,128)S(1)}, f32[1,8,256]{2,1,0:T(8,128)S(1)}, f32[1,8]{1,0:T(1,128)S(1)}) custom-call(bf16[2,32,128]{2,1,0:T(8,128)(2,1)} %inputs_hbm.1, bf16[3076,128]{1,0:T(8,128)(2,1)} %bitcast.2, f32[2,8]{1,0:T(2,128)} %bias_hbm.1, f32[1,8,256,512]{3,2,1,0:T(8,128)} %memory_hbm.1, ...), custom_call_target="tpu_custom_call" | custom-call | tf_op jit(solution)/shard_map/pallas_call | solution.py:400
  31.7 2.1 %shard_map.112 = (bf16[2,32,128]{2,1,0:T(8,128)(2,1)}, f32[1,8,256,512]{3,2,1,0:T(8,128)}, f32[1,8,256]{2,1,0:T(8,128)}, f32[1,8]{1,0:T(1,128)}) custom-call(bf16[2,32,128]{2,1,0:T(8,128)(2,1)S(1)} %get-tuple-element.8.mixed, f32[1,8,256,512]{3,2,1,0:T(8,128)S(1)} %get-tuple-element.9.memory, f32[1,8,256]{2,1,0:T(8,128)S(1)} %get-tuple-element.10.norm, ...), custom_call_target="tpu_custom_call" | custom-call | tf_op jit(solution)/shard_map/pallas_call | solution.py:457

commit v6 on v5

--- a/solution.py
+++ b/solution.py
@@ -67,7 +67,7 @@
             (bias_hbm, bias),
             (stab_hbm, stab),
             (norm_hbm.at[0], norm),
-            (gain_hbm, gain),
+            (gain_hbm, gain.at[pl.ds(0, 32)]),
             (memory_hbm.at[0], memory),
             (out_weight_hbm, out_weight),
         ))
@@ -409,23 +409,23 @@
             pltpu.VMEM((2, 8), F32),
             pltpu.VMEM((8, 256), F32),
             pltpu.VMEM((1, 8), F32),
-            pltpu.VMEM((32, 128), F32),
+            pltpu.VMEM((40, 128), F32),
             pltpu.VMEM((2, 2, 32, 128), BF16),
             pltpu.VMEM((8, 2, 2, 32, 128), BF16),
             pltpu.VMEM((4, 16, 128), BF16),
             pltpu.VMEM((16, 128), F32),
             pltpu.VMEM((2, 2, 384, 512), BF16),
-            pltpu.VMEM((2, 1024, 128), F32),
+            pltpu.VMEM((2, 1040, 128), F32),
             pltpu.VMEM((2, 64, 16, 128), BF16),
             pltpu.VMEM((2, 64, 16, 128), BF16),
             pltpu.VMEM((96, 128), F32),
             pltpu.VMEM((104, 128), F32),
-            pltpu.VMEM((2, 96, 128), F32),
+            pltpu.VMEM((2, 104, 128), F32),
             pltpu.VMEM((8, 512), F32),
             pltpu.VMEM((2, 8, 512), F32),
             pltpu.VMEM((2, 32, 128), BF16),
             pltpu.VMEM((2, 32, 32, 128), BF16),
-            pltpu.VMEM((1024, 128), F32),
+            pltpu.VMEM((1056, 128), F32),
             pltpu.VMEM((32, 4096), BF16),
             dma((8,)),
             dma,

time: 34.3 us -> 34.3 us (level)
  no operation moved by 1% of the time
where the time goes in v6:
time: 34.3 us; the launch traced here: 33.8 us
  Pallas kernels  33.1 us (97%)
  between operations  0.64 us (2%)
    pallas_call x1, Pallas kernels, body(): pl.pallas_call(exchange_kernel, out_shape=out_shape, in_specs=[hbm] * 8,...  31 us
    pallas_call x1, Pallas kernels, body(): pl.pallas_call(hand_over_kernel, out_shape=out_shape, in_specs=[vmem] * 4...  2.11 us

profile of v6, /device:TPU:1, one launch (start us, length us, event | category | flops | bytes accessed | tf_op | source)
XLA Modules:
  0.0 33.8 jit_solution(13438458018103204651)
XLA Ops:
  0.6 31.0 %shard_map.111 = (bf16[2,32,128]{2,1,0:T(8,128)(2,1)S(1)}, f32[1,8,256,512]{3,2,1,0:T(8,128)S(1)}, f32[1,8,256]{2,1,0:T(8,128)S(1)}, f32[1,8]{1,0:T(1,128)S(1)}) custom-call(bf16[2,32,128]{2,1,0:T(8,128)(2,1)} %inputs_hbm.1, bf16[3076,128]{1,0:T(8,128)(2,1)} %bitcast.2, f32[2,8]{1,0:T(2,128)} %bias_hbm.1, f32[1,8,256,512]{3,2,1,0:T(8,128)} %memory_hbm.1, ...), custom_call_target="tpu_custom_call" | custom-call | tf_op jit(solution)/shard_map/pallas_call | solution.py:400
  31.7 2.1 %shard_map.112 = (bf16[2,32,128]{2,1,0:T(8,128)(2,1)}, f32[1,8,256,512]{3,2,1,0:T(8,128)}, f32[1,8,256]{2,1,0:T(8,128)}, f32[1,8]{1,0:T(1,128)}) custom-call(bf16[2,32,128]{2,1,0:T(8,128)(2,1)S(1)} %get-tuple-element.8.mixed, f32[1,8,256,512]{3,2,1,0:T(8,128)S(1)} %get-tuple-element.9.memory, f32[1,8,256]{2,1,0:T(8,128)S(1)} %get-tuple-element.10.norm, ...), custom_call_target="tpu_custom_call" | custom-call | tf_op jit(solution)/shard_map/pallas_call | solution.py:457

commit v7 on v6

--- a/solution.py
+++ b/solution.py
@@ -30,7 +30,7 @@
     inputs_hbm, weight_hbm, bias_hbm, memory_hbm, norm_hbm, stab_hbm, gain_hbm, out_weight_hbm,
     mixed_ref, memory_out_ref, norm_out_ref, stab_out_ref,
     stage, memory, out_weight, bias, norm, stab, gain, rows_in, rows, tail, tail_f32, weights,
-    send_f32, send, received, tiles, rolled, flat, numer, scaled, readout, gathered, gathered_f32, left,
+    send_f32, send, received, tiles, rolled, flat, numer, scaled, readout, gathered, gathered_f32,
     load_sem, own_sem, rows_send, rows_sem, ring_send, ring_sem, tail_send, tail_sem, w_send, w_sem, pass_send,
     pass_sem, sums_send, sums_recv, gather_send, gather_recv, ping_sem,
 ):
@@ -358,11 +358,18 @@
         for block in range(4):
             piece = gathered[draft, pl.ds(block * 8, 8)].reshape(256, 128)
             gathered_f32[pl.ds(block * 256, 256), :] = piece.astype(F32)
-        for j in range(4):
-            for head in range(8):
-                piece = gathered_f32[pl.ds(j * 8 + head, 32, stride=32), :]
-                left[:, pl.ds((head * 4 + j) * 128, 128)] = piece.astype(BF16)
-        product = jnp.dot(left[...], out_weight[...], preferred_element_type=F32)
+        product = None
+        for half in range(2):
+            pieces_of_half = [
+                gathered_f32[pl.ds(j * 8 + head, 32, stride=32), :].astype(BF16)
+                for head in range(half * 4, half * 4 + 4)
+                for j in range(4)
+            ]
+            term = jnp.dot(
+                jnp.concatenate(pieces_of_half, axis=1), out_weight[pl.ds(half * 2048, 2048), :],
+                preferred_element_type=F32,
+            )
+            product = term if product is None else product + term
         mixed_ref[draft] = product.astype(BF16)
 
     rows_copy.wait_send()
@@ -426,7 +433,6 @@
             pltpu.VMEM((2, 32, 128), BF16),
             pltpu.VMEM((2, 32, 32, 128), BF16),
             pltpu.VMEM((1056, 128), F32),
-            pltpu.VMEM((32, 4096), BF16),
             dma((8,)),
             dma,
             dma,

time: 34.3 us -> 34.3 us (level)
  no operation moved by 1% of the time
where the time goes in v7:
time: 34.3 us; the launch traced here: 33.7 us
  Pallas kernels  33 us (96%)
  between operations  0.64 us (2%)
    pallas_call x1, Pallas kernels, body(): pl.pallas_call(exchange_kernel, out_shape=out_shape, in_specs=[hbm] * 8,...  30.9 us
    pallas_call x1, Pallas kernels, body(): pl.pallas_call(hand_over_kernel, out_shape=out_shape, in_specs=[vmem] * 4...  2.11 us

profile of v7, /device:TPU:1, one launch (start us, length us, event | category | flops | bytes accessed | tf_op | source)
XLA Modules:
  0.0 33.7 jit_solution(38178911622682230)
XLA Ops:
  0.6 30.9 %shard_map.111 = (bf16[2,32,128]{2,1,0:T(8,128)(2,1)S(1)}, f32[1,8,256,512]{3,2,1,0:T(8,128)S(1)}, f32[1,8,256]{2,1,0:T(8,128)S(1)}, f32[1,8]{1,0:T(1,128)S(1)}) custom-call(bf16[2,32,128]{2,1,0:T(8,128)(2,1)} %inputs_hbm.1, bf16[3076,128]{1,0:T(8,128)(2,1)} %bitcast.2, f32[2,8]{1,0:T(2,128)} %bias_hbm.1, f32[1,8,256,512]{3,2,1,0:T(8,128)} %memory_hbm.1, ...), custom_call_target="tpu_custom_call" | custom-call | tf_op jit(solution)/shard_map/pallas_call | solution.py:407
  31.6 2.1 %shard_map.112 = (bf16[2,32,128]{2,1,0:T(8,128)(2,1)}, f32[1,8,256,512]{3,2,1,0:T(8,128)}, f32[1,8,256]{2,1,0:T(8,128)}, f32[1,8]{1,0:T(1,128)}) custom-call(bf16[2,32,128]{2,1,0:T(8,128)(2,1)S(1)} %get-tuple-element.8.mixed, f32[1,8,256,512]{3,2,1,0:T(8,128)S(1)} %get-tuple-element.9.memory, f32[1,8,256]{2,1,0:T(8,128)S(1)} %get-tuple-element.10.norm, ...), custom_call_target="tpu_custom_call" | custom-call | tf_op jit(solution)/shard_map/pallas_call | solution.py:463
